TPU v7x, 32 devices: a whole 2x2x4 slice. The times are simulated.
32 devices in a mesh: slab: 2 (over y), space: 16 (over z, x, core).
Axes of the slice: x: 2, y: 2, z: 4, core: 2. Of those that a mesh axis runs over, the one named last changes fastest.
Arguments:
- snapshots: bfloat16 [2048, 16384], P('space', 'slab'), parts along dimension 1, may hold values from -40 to 40
- weights: float32 [16384], P(('slab', 'space')), parts along dimension 0, may hold values from 0.2 to 2
Outputs:
- modes: bfloat16 [2, 129, 15, 16384], P(None, None, None, ('slab', 'space')), parts along dimension 3
There are 2 independent parts, one for each index of `slab`. A program takes and returns all parts, laid end to end along the dimension named above; each array names one. Nothing has to cross between parts.
All inputs are finite; a program needn't handle non-finite values.
Results may differ from a plain program's by a relative error of at most 0.0063.
Values may be sent and summed in bfloat16 or wider, within the bound.
A program may use at most 64 MiB of HBM per device.

v0:
```python
import math

import jax
import jax.numpy as jnp
from jax import lax
from jax.sharding import PartitionSpec as P

SEGMENT_SAMPLES = 256
NB = 15
FREQS = 129


def make_table():
    sample_moments = jnp.arange(SEGMENT_SAMPLES, dtype=jnp.int32)
    overtone_multiples = jnp.arange(FREQS, dtype=jnp.int32)
    angle_position = overtone_multiples[:, None] * sample_moments[None, :] % SEGMENT_SAMPLES
    phases = 2.0 * math.pi * angle_position.astype(jnp.float32) / SEGMENT_SAMPLES
    taper_weights = 0.5 - 0.5 * jnp.cos(
        2.0 * math.pi * sample_moments.astype(jnp.float32) / SEGMENT_SAMPLES
    )
    scaling = 1.0 / math.sqrt(3.0 * SEGMENT_SAMPLES / 8.0)
    table = jnp.stack(
        (taper_weights * jnp.cos(phases) * scaling, -taper_weights * jnp.sin(phases) * scaling)
    )
    table = table.reshape(2 * FREQS, SEGMENT_SAMPLES).astype(jnp.bfloat16)
    row_sums = jnp.sum(table, axis=1, dtype=jnp.float32)
    return (table, row_sums)


def spectra_of(series, table, row_sums):
    count_snaps, cell_count = series.shape
    average = jnp.sum(series, axis=0, dtype=jnp.float32) / count_snaps
    halves = series.reshape(count_snaps // (SEGMENT_SAMPLES // 2), SEGMENT_SAMPLES // 2, cell_count)
    blocks = jnp.concatenate((halves[:-1], halves[1:]), axis=1)
    spectra = jnp.einsum("kt,btc->kbc", table, blocks, preferred_element_type=jnp.float32)
    spectra = spectra - row_sums[:, None, None] * average[None, None, :]
    return spectra.reshape(2, FREQS, NB, cell_count)


def gram_parts(weighted):
    products = jnp.einsum(
        "pfac,qfbc->fpaqb", weighted, weighted, preferred_element_type=jnp.float32
    )
    real_part = products[:, 0, :, 0, :] + products[:, 1, :, 1, :]
    imag_part = products[:, 0, :, 1, :] - products[:, 1, :, 0, :]
    return jnp.stack((real_part, imag_part))


def invert_definite(system):
    order = system.shape[1]
    identity_big = jnp.broadcast_to(jnp.eye(order, dtype=jnp.float32), system.shape)
    augmented = jnp.concatenate((system, identity_big), axis=2)
    for step in range(order):
        pivot_row = augmented[:, step, :] / augmented[:, step, step][:, None]
        column = augmented[:, :, step]
        augmented = augmented - column[:, :, None] * pivot_row[:, None, :]
        augmented = augmented.at[:, step, :].set(pivot_row)
    return augmented[:, :, order:]


def filter_of(gram):
    real_part, imag_part = (gram[0], gram[1])
    level = jnp.trace(real_part, axis1=1, axis2=2) / NB
    identity = jnp.eye(NB, dtype=jnp.float32)
    shifted = real_part + level[:, None, None] * identity
    system = jnp.concatenate(
        (
            jnp.concatenate((shifted, -imag_part), axis=2),
            jnp.concatenate((imag_part, shifted), axis=2),
        ),
        axis=1,
    )
    identity_big = jnp.broadcast_to(jnp.eye(2 * NB, dtype=jnp.float32), system.shape)
    inverse = invert_definite(system)
    return (identity_big - level[:, None, None] * inverse).astype(jnp.bfloat16)


def per_device(snapshots, weights):
    devices = lax.axis_size("space")
    local_cells = snapshots.shape[1] // devices
    table, row_sums = make_table()
    shaped = snapshots.reshape(snapshots.shape[0], devices, local_cells)
    columns = lax.all_to_all(shaped, "space", split_axis=1, concat_axis=0, tiled=True)
    spectra = spectra_of(columns[:, 0, :], table, row_sums)
    root_weight = jnp.sqrt(weights)
    weighted = (spectra * root_weight).astype(jnp.bfloat16)
    partial_gram = gram_parts(weighted)
    total_gram = lax.psum(partial_gram, "space")
    filters = filter_of(total_gram)
    filters_five = filters.reshape(FREQS, 2, NB, 2, NB)
    mixed = jnp.einsum(
        "fpaqb,pfac->qfbc", filters_five, weighted, preferred_element_type=jnp.float32
    )
    return (mixed / root_weight).astype(jnp.bfloat16)


def solution(mesh):
    return jax.shard_map(
        per_device,
        mesh=mesh,
        in_specs=(P("space", "slab"), P(("slab", "space"))),
        out_specs=P(None, None, None, ("slab", "space")),
        check_vma=False,
    )
```

profile of v0, /device:TPU:0, one launch (start us, length us, event | category | flops | bytes accessed | tf_op | source)
XLA Modules:
  0.0 216.9 jit_solution(5388319800626112902)
XLA Ops:
  6.5 3.2 %copy.139 = bf16[128,8192]{0,1:T(8,128)(2,1)S(1)} copy(bf16[128,8192]{1,0:T(8,128)(2,1)} %param.62) | data formatting | bytes 4194304 | tf_op args[0]
  9.8 2.6 %copy.140 = bf16[128,16,512]{2,0,1:T(8,128)(2,1)} copy(bf16[128,16,512]{0,2,1:T(8,128)(2,1)S(1)} %bitcast.229) | data formatting | bytes 4194304 | tf_op jit(solution)/shard_map/reshape | solution.py:82
  12.4 7.5 %all-to-all-start = ((bf16[128,16,512]{2,0,1:T(8,128)(2,1)}), bf16[128,16,512]{2,0,1:T(8,128)(2,1)S(1)}, u32[]{:S(2)}, u32[]{:S(2)}) async-start(bf16[128,16,512]{2,0,1:T(8,128)(2,1)} %copy.140), calls=%async_computation | async-start | bytes 4194304 | tf_op jit(solution)/shard_map/all_to_all | solution.py:83
  20.0 0.6 multiply_multiply_fusion
  20.9 40.1 %all-to-all-done = bf16[128,16,512]{2,0,1:T(8,128)(2,1)S(1)} async-done(((bf16[128,16,512]{2,0,1:T(8,128)(2,1)}), bf16[128,16,512]{2,0,1:T(8,128)(2,1)S(1)}, u32[]{:S(2)}, u32[]{:S(2)}) %all-to-all-start) | async-done | bytes 2097184 | tf_op jit(solution)/shard_map/all_to_all | solution.py:83
  61.0 0.3 convert_reduce_fusion
  61.3 0.4 slice_bitcast_fusion.1
  61.9 1.8 broadcast_subtract_fusion
  63.6 4.6 %copy.141 = f32[258,15,512]{2,1,0:T(8,128)S(1)} copy(f32[258,15,512]{2,0,1:T(8,128)S(1)} %broadcast_subtract_fusion) | data formatting | bytes 15851520 | tf_op jit(solution)/shard_map/sub | solution.py:36
  68.3 6.1 %fusion.2 = f32[129,2,15,2,15]{4,2,3,1,0:T(8,128)S(1)} fusion(f32[2,129,15,512]{3,2,1,0:T(8,128)S(1)} %bitcast.226, f32[512]{0:T(512)S(1)} %sqrt.3), kind=kOutput, calls=%fused_computation.4 | convolution fusion | flops 126812160 | bytes 8392208 | tf_op jit(solution)/shard_map/pfac,qfbc->fpaqb/dot_general | solution.py:41
  74.4 1.3 fusion.17
  75.6 1.8 copy.144
  77.5 0.7 copy.145
  78.1 1.2 pad_maximum_fusion.1
  79.4 96.4 %all-reduce.2.cloned.1.call-done = f32[2,129,15,15]{1,0,3,2:T(2,128)} async-done(((f32[2,129,15,15]{1,0,3,2:T(2,128)}), f32[2,129,15,15]{1,0,3,2:T(2,128)}) %all-reduce.2.cloned.1.call-update) | async-done | bytes 232216 | tf_op jit(solution)/shard_map/psum | solution.py:88
  175.8 1.6 fusion.93
  177.9 0.3 pad_maximum_fusion
  178.3 0.4 multiply_subtract_fusion.29
  179.1 0.3 multiply_subtract_fusion.27
  179.5 0.3 multiply_subtract_fusion.26
  180.3 0.5 multiply_subtract_fusion.24
  180.9 0.3 multiply_subtract_fusion.23
  181.8 0.3 multiply_subtract_fusion.21
  183.0 0.3 multiply_subtract_fusion.18
  184.6 0.3 multiply_subtract_fusion.14
  185.4 0.3 multiply_subtract_fusion.12
  186.7 0.3 multiply_subtract_fusion.9
  189.1 0.3 multiply_subtract_fusion.3
  190.3 0.3 multiply_subtract_fusion
  191.1 4.2 %copy.148 = bf16[129,2,15,2,15]{2,4,1,3,0:T(8,128)(2,1)S(1)} copy(bf16[129,2,15,2,15]{0,4,3,2,1:T(8,128)(2,1)S(1)} %reshape.1499) | data formatting | bytes 464400 | tf_op jit(solution)/shard_map/reshape | solution.py:90
  195.3 4.8 %fusion.4 = bf16[2,129,15,512]{3,2,0,1:T(8,128)(2,1)S(1)} fusion(f32[512]{0:T(512)S(1)} %sqrt.3, bf16[129,2,15,2,15]{2,4,1,3,0:T(8,128)(2,1)S(1)} %copy.148, f32[2,129,15,512]{3,2,1,0:T(8,128)} %bitcast.227), kind=kOutput, calls=%fused_computation.6 | convolution fusion | flops 126812160 | bytes 12122888 | tf_op jit(solution)/shard_map/fpaqb,pfac->qfbc/dot_general | solution.py:91
  200.2 9.9 %copy.149 = bf16[2,129,15,512]{3,0,2,1:T(2,128)(2,1)} copy(bf16[2,129,15,512]{3,2,0,1:T(8,128)(2,1)S(1)} %fusion.4) | data formatting | bytes 7925760 | tf_op jit(solution)/shard_map/convert_element_type | solution.py:94
  (193 shorter events, 8.7 us)
Async XLA Ops:
  12.4 8.5 %copy-start.1 = (f32[512]{0:T(512)S(1)}, f32[512]{0:T(512)}, u32[]{:S(2)}) copy-start(f32[512]{0:T(512)} %param.63) | copy-start | bytes 6148
  12.4 48.6 %all-to-all-start = ((bf16[128,16,512]{2,0,1:T(8,128)(2,1)}), bf16[128,16,512]{2,0,1:T(8,128)(2,1)S(1)}, u32[]{:S(2)}, u32[]{:S(2)}) async-start(bf16[128,16,512]{2,0,1:T(8,128)(2,1)} %copy.140), calls=%async_computation | async-start | bytes 4194304 | tf_op jit(solution)/shard_map/all_to_all | solution.py:83
  19.9 156.0 %all-reduce.2.cloned.1.call-start = ((), (), s32[]{:S(2)}) async-start(), calls=%async_computation.1 | async-start | bytes 921600 | tf_op jit(solution)/shard_map/psum | solution.py:88
  68.3 6.1 %copy-start = (f32[258,15,512]{2,1,0:T(8,128)}, f32[258,15,512]{2,1,0:T(8,128)S(1)}, u32[]{:S(2)}) copy-start(f32[258,15,512]{2,1,0:T(8,128)S(1)} %copy.141) | copy-start | bytes 23777284
Sparse Core Ops, SparseCore 0:
  79.5 96.2 all-reduce.1
where the time goes:
time: 217 us
  waiting for transfers between devices  136 us (63%)
  local copies, waits for them, and re-layouts  30.7 us (14%)
  between operations  15 us (7%)
  other arithmetic  14.6 us (7%)
  matrix products  12.7 us (6%)
  starting transfers between devices  7.53 us (3%)
    psum x1, waiting for transfers between devices, per_device(): total_gram = lax.psum(partial_gram, 'space')  96.4 us
    all_to_all x1, waiting for transfers between devices, per_device(): lax.all_to_all(shaped, 'space', split_axis=1, concat_axis=0, tiled=True)  40.1 us
    convert_element_type x1, local copies, waits for them, and re-layouts, per_device(): return (mixed / root_weight).astype(jnp.bfloat16)  9.88 us
    sub x30, other arithmetic, invert_definite(): augmented = augmented - column[:, :, None] * pivot_row[:, None, :]  9.24 us
    all_to_all x1, starting transfers between devices, per_device(): lax.all_to_all(shaped, 'space', split_axis=1, concat_axis=0, tiled=True)  7.49 us
    dot_general x1, matrix products, gram_parts(): jnp.einsum('pfac,qfbc->fpaqb', weighted, weighted, preferred_element_type...  6.07 us
    dot_general x1, matrix products, per_device(): jnp.einsum('fpaqb,pfac->qfbc', filters_five, weighted, preferred_element_...  4.84 us
    sub x1, local copies, waits for them, and re-layouts, spectra_of(): spectra = spectra - row_sums[:, None, None] * average[None, None, :]  4.62 us
  transfers between devices with their start and end apart: 2, of which 2 were waited for; matrix products, arithmetic and copies ran while one was open for 0% of the time, Pallas kernels for 0%

commit v1 on v0

v1 whole, which is shorter than its diff:
```python
import functools
import math

import jax
import jax.numpy as jnp
import numpy as np
import ml_dtypes
from jax import lax
from jax.experimental import pallas as pl
from jax.experimental.pallas import tpu as pltpu
from jax.sharding import PartitionSpec as P

SEG = 256
HALF = SEG // 2
NB = 15
FREQS = 129
NBP = 16
GROUP = 8
GROUPS = -(-FREQS // GROUP)
FP = GROUPS * GROUP
LANES = 128
MESH = pl.DeviceIdType.MESH
VMEM = pl.BlockSpec(memory_space=pltpu.VMEM)


def make_table():
    t = np.arange(SEG)
    k = np.arange(FREQS)
    phases = 2.0 * np.pi * (k[:, None] * t[None, :] % SEG) / SEG
    taper = 0.5 - 0.5 * np.cos(2.0 * np.pi * t / SEG)
    scaling = 1.0 / math.sqrt(3.0 * SEG / 8.0)
    table = np.zeros((2, FP, SEG), np.float32)
    table[0, :FREQS] = taper * np.cos(phases) * scaling
    table[1, :FREQS] = -taper * np.sin(phases) * scaling
    return table.reshape(2 * FP, SEG).astype(ml_dtypes.bfloat16)


def gram_rows(n):
    return -(-(GROUPS * 2 * NBP // 8) // n) * 8


def dft_chunk(tab_ref, x_ref, w_ref, s_ref, lane0, width):
    tab = tab_ref[...]
    row_sums = jnp.sum(tab.astype(jnp.float32), axis=1, keepdims=True)
    cols = pl.ds(lane0, width)
    average = jnp.sum(x_ref[:, cols].astype(jnp.float32), axis=0, keepdims=True) / x_ref.shape[0]
    root = jnp.sqrt(w_ref[:, cols])
    corr = row_sums * (average * root)
    for b in range(NB):
        sp = jnp.dot(tab, x_ref[b * HALF : b * HALF + SEG, cols], preferred_element_type=jnp.float32)
        sp = sp * root - corr
        for p in range(2):
            for i in range(width // LANES):
                s_ref[p, lane0 // LANES + i, pl.ds(b, FP, stride=NBP), :] = sp[
                    p * FP : (p + 1) * FP, i * LANES : (i + 1) * LANES
                ]
    for p in range(2):
        for i in range(width // LANES):
            s_ref[p, lane0 // LANES + i, pl.ds(NB, FP, stride=NBP), :] = jnp.zeros((FP, LANES), jnp.float32)


def gram_group(s_ref, wtd_ref, g_ref, chunks, g):
    rows = pl.ds(pl.multiple_of(g * LANES, LANES), LANES)
    parts = [
        jnp.concatenate([s_ref[p, i, rows, :] for i in range(chunks)], axis=1).astype(jnp.bfloat16)
        for p in range(2)
    ]
    for p in range(2):
        wtd_ref[p, pl.ds(pl.multiple_of(g * GROUP, GROUP), GROUP)] = parts[p].reshape(
            GROUP, NBP, chunks * LANES
        )
    x = jnp.concatenate(parts, axis=0)
    prod = lax.dot_general(x, x, (((1,), (1,)), ((), ())), preferred_element_type=jnp.float32)
    re = prod[:LANES, :LANES] + prod[LANES:, LANES:]
    im = prod[:LANES, LANES:] - prod[LANES:, :LANES]
    freq = lax.broadcasted_iota(jnp.int32, (NBP, LANES), 1) // NBP
    for part, full in enumerate((re, im)):
        folded = jnp.zeros((NBP, LANES), jnp.float32)
        for k in range(GROUP):
            folded = jnp.where(freq == k, full[k * NBP : (k + 1) * NBP], folded)
        g_ref[pl.ds(pl.multiple_of(g * 2 * NBP + part * NBP, NBP), NBP), :] = folded


def spectra_kernel(tab_ref, x_ref, w_ref, wtd_ref, g_ref, s_ref):
    cells = x_ref.shape[1]
    for lane0 in range(0, cells, 256):
        dft_chunk(tab_ref, x_ref, w_ref, s_ref, lane0, 256)
    used = GROUPS * 2 * NBP
    if g_ref.shape[0] > used:
        g_ref[used:, :] = jnp.zeros((g_ref.shape[0] - used, LANES), jnp.float32)

    @pl.loop(0, GROUPS)
    def _(g):
        gram_group(s_ref, wtd_ref, g_ref, cells // LANES, g)


def sum_kernel(n, g_ref, out_ref, got_ref, own_ref, send1, recv1, send2, recv2):
    me = lax.axis_index("space")
    share = g_ref.shape[0] // n
    mine = pl.ds(pl.multiple_of(me * share, 8), share)

    def peer(i):
        return lax.rem(me + i, n)

    barrier = pltpu.get_barrier_semaphore()

    @pl.loop(1, n)
    def _(i):
        pl.semaphore_signal(barrier, inc=1, device_id={"space": peer(i)}, device_id_type=MESH)

    pl.semaphore_wait(barrier, n - 1)

    def scatter(i):
        there = peer(i)
        return pltpu.make_async_remote_copy(
            src_ref=g_ref.at[pl.ds(pl.multiple_of(there * share, 8), share)],
            dst_ref=got_ref.at[i],
            send_sem=send1.at[i],
            recv_sem=recv1.at[i],
            device_id={"space": there},
            device_id_type=MESH,
        )

    def gather(i):
        return pltpu.make_async_remote_copy(
            src_ref=own_ref,
            dst_ref=out_ref.at[mine],
            send_sem=send2.at[i],
            recv_sem=recv2.at[i],
            device_id={"space": peer(i)},
            device_id_type=MESH,
        )

    @pl.loop(1, n)
    def _(i):
        scatter(i).start()

    own_ref[...] = g_ref[mine, :]

    @pl.loop(1, n)
    def _(i):
        scatter(i).wait_recv()
        own_ref[...] += got_ref[i]

    @pl.loop(1, n)
    def _(i):
        gather(i).start()

    out_ref[mine, :] = own_ref[...]

    @pl.loop(1, n)
    def _(i):
        scatter(i).wait_send()
        gather(i).wait()


def group_sum(x, lane):
    for step in (1, 2, 4, 8):
        x = x + jnp.take_along_axis(x, jnp.bitwise_xor(lane, step), axis=1)
    return x


def invert(g_ref, f_ref):
    shape = (GROUPS, NBP, LANES)
    flat = (GROUPS * NBP, LANES)
    packed = g_ref[: GROUPS * 2 * NBP, :].reshape(GROUPS, 2, NBP, LANES)
    re, im = packed[:, 0], packed[:, 1]
    row = lax.broadcasted_iota(jnp.int32, (1, NBP, LANES), 1)
    lane = lax.broadcasted_iota(jnp.int32, (1, NBP, LANES), 2)
    col = lane % NBP
    lane_flat = lax.broadcasted_iota(jnp.int32, flat, 1)
    base = lane_flat - lane_flat % NBP
    diag = row == col
    trace = jnp.sum(jnp.where(diag, re, 0.0), axis=1, keepdims=True)
    level = group_sum(jnp.broadcast_to(trace, shape).reshape(flat), lane_flat).reshape(shape) / NB
    group = lax.broadcasted_iota(jnp.int32, shape, 0)
    real = group * GROUP + lax.broadcasted_iota(jnp.int32, shape, 2) // NBP < FREQS
    level = jnp.where(real, level, 1.0)
    re = re + jnp.where(diag, level, 0.0)
    for j in range(NB):
        index = base + j
        col_re = jnp.take_along_axis(re.reshape(flat), index, axis=1).reshape(shape)
        col_im = jnp.take_along_axis(im.reshape(flat), index, axis=1).reshape(shape)
        inverse = 1.0 / col_re[:, j : j + 1]
        here = (col == j)[:, j : j + 1]
        row_re = jnp.where(here, inverse, re[:, j : j + 1] * inverse)
        row_im = jnp.where(here, 0.0, im[:, j : j + 1] * inverse)
        cross = (row == j) | (col == j)
        col_re = jnp.where(row == j, -1.0, col_re)
        col_im = jnp.where(row == j, 0.0, col_im)
        re = jnp.where(cross, 0.0, re) - (col_re * row_re - col_im * row_im)
        im = jnp.where(cross, 0.0, im) - (col_re * row_im + col_im * row_re)
    f_ref[:, 0] = jnp.where(diag, 1.0, 0.0) - level * re
    f_ref[:, 1] = level * im


def modes_kernel(g_ref, w_ref, wtd_ref, out_ref, f_ref):
    g = pl.program_id(0)

    @pl.when(g == 0)
    def _():
        invert(g_ref, f_ref)

    cells = w_ref.shape[1]
    inverse_root = 1.0 / jnp.sqrt(w_ref[...])
    own = (
        lax.broadcasted_iota(jnp.int32, (LANES, LANES), 0) // NBP
        == lax.broadcasted_iota(jnp.int32, (LANES, LANES), 1) // NBP
    )
    same = jnp.where(own, jnp.concatenate([f_ref[g, 0]] * GROUP, axis=0), 0.0).astype(jnp.bfloat16)
    other = jnp.where(own, jnp.concatenate([f_ref[g, 1]] * GROUP, axis=0), 0.0).astype(jnp.bfloat16)
    filters = jnp.concatenate(
        (jnp.concatenate((same, other), axis=1), jnp.concatenate((-other, same), axis=1)), axis=0
    )
    wtd = wtd_ref[...].reshape(2 * LANES, cells)
    mixed = jnp.dot(filters, wtd, preferred_element_type=jnp.float32) * inverse_root
    mixed = mixed.astype(jnp.bfloat16).reshape(2, GROUP, NBP, cells)
    out_ref[...] = mixed[:, :, :NB]


def per_device(snapshots, weights):
    n = lax.axis_size("space")
    cells = snapshots.shape[1] // n
    table = jnp.asarray(make_table())
    shaped = snapshots.reshape(snapshots.shape[0], n, cells)
    columns = lax.all_to_all(shaped, "space", split_axis=1, concat_axis=0, tiled=True)
    x = columns[:, 0, :]
    w = weights.reshape(1, cells)
    share = gram_rows(n)
    wtd, gram = pl.pallas_call(
        spectra_kernel,
        out_shape=(
            jax.ShapeDtypeStruct((2, FP, NBP, cells), jnp.bfloat16),
            jax.ShapeDtypeStruct((n * share, LANES), jnp.float32),
        ),
        in_specs=[VMEM] * 3,
        out_specs=(VMEM, VMEM),
        scratch_shapes=[pltpu.VMEM((2, cells // LANES, FP * NBP, LANES), jnp.float32)],
        compiler_params=pltpu.CompilerParams(vmem_limit_bytes=40 << 20),
        name="spectra",
    )(table, x, w)
    total = pl.pallas_call(
        functools.partial(sum_kernel, n),
        out_shape=jax.ShapeDtypeStruct((n * share, LANES), jnp.float32),
        in_specs=[VMEM],
        out_specs=VMEM,
        scratch_shapes=[
            pltpu.VMEM((n, share, LANES), jnp.float32),
            pltpu.VMEM((share, LANES), jnp.float32),
        ]
        + [pltpu.SemaphoreType.DMA((n,))] * 4,
        compiler_params=pltpu.CompilerParams(collective_id=0, has_side_effects=True),
        name="gram_sum",
    )(gram)
    return pl.pallas_call(
        modes_kernel,
        grid=(GROUPS,),
        out_shape=jax.ShapeDtypeStruct((2, FREQS, NB, cells), jnp.bfloat16),
        in_specs=[
            VMEM,
            VMEM,
            pl.BlockSpec((2, GROUP, NBP, cells), lambda g: (0, g, 0, 0)),
        ],
        out_specs=pl.BlockSpec((2, GROUP, NB, cells), lambda g: (0, g, 0, 0)),
        scratch_shapes=[pltpu.VMEM((GROUPS, 2, NBP, LANES), jnp.float32)],
        compiler_params=pltpu.CompilerParams(vmem_limit_bytes=32 << 20),
        name="modes",
    )(total, w, wtd)


def solution(mesh):
    return jax.shard_map(
        per_device,
        mesh=mesh,
        in_specs=(P("space", "slab"), P(("slab", "space"))),
        out_specs=P(None, None, None, ("slab", "space")),
        check_vma=False,
    )
```

time: 217 us -> 109 us (0.50)
  waiting for transfers between devices: 136 us -> 0 us
  blocking collectives: 0 us -> 54.5 us
  Pallas kernels: 0 us -> 35.9 us
  between operations: 15 us -> 0.05 us
  other arithmetic: 14.6 us -> 0 us
  local copies, waits for them, and re-layouts: 30.7 us -> 17.7 us
  matrix products: 12.7 us -> 0 us
  starting transfers between devices: 7.53 us -> 0 us
    psum x1 -> x0, waiting for transfers between devices: 96.4 us -> none  [per_device(): total_gram = lax.psum(partial_gram, 'space')]
    all_to_all x0 -> x1, blocking collectives: none -> 54.5 us  [per_device(): lax.all_to_all(shaped, 'space', split_axis=1, concat_axis=0, tiled=True)]
    all_to_all x1 -> x0, waiting for transfers between devices: 40.1 us -> none  [per_device(): lax.all_to_all(shaped, 'space', split_axis=1, concat_axis=0, tiled=True)]
    pallas_call x0 -> x3, Pallas kernels: none -> 35.9 us  [the longest x1 19.8 us: per_device(): pl.pallas_call(functools.partial(sum_kernel, n), out_shape=jax.ShapeDtype...]
    dot_general x3 -> x0, matrix products: 12.7 us -> none  [the longest x1 6.07 us: gram_parts(): jnp.einsum('pfac,qfbc->fpaqb', weighted, weighted, preferred_element_type...]
    convert_element_type x2 -> x0, local copies, waits for them, and re-layouts: 9.92 us -> none  [the longest x1 9.88 us: per_device(): return (mixed / root_weight).astype(jnp.bfloat16)]
    pallas_call x0 -> x1, local copies, waits for them, and re-layouts: none -> 9.88 us  [per_device(): pl.pallas_call(modes_kernel, grid=(GROUPS,), out_shape=jax.ShapeDtypeStru...]
    sub x31 -> x0, other arithmetic: 9.28 us -> none  [the longest x30 9.24 us: invert_definite(): augmented = augmented - column[:, :, None] * pivot_row[:, None, :]]
  transfers between devices with their start and end apart: 2 -> 0, of which waited for: 2 -> 0; matrix products, arithmetic and copies ran while one was open for 0% -> 0% of each run, Pallas kernels for 0% -> 0%
where the time goes in v1:
time: 109 us; the launch traced here: 108 us
  blocking collectives  54.5 us (50%)
  Pallas kernels  35.9 us (33%)
  local copies, waits for them, and re-layouts  17.7 us (16%)
    all_to_all x1, blocking collectives, per_device(): lax.all_to_all(shaped, 'space', split_axis=1, concat_axis=0, tiled=True)  54.5 us
    pallas_call x1, Pallas kernels, per_device(): pl.pallas_call(functools.partial(sum_kernel, n), out_shape=jax.ShapeDtype...  19.8 us
    pallas_call x1, local copies, waits for them, and re-layouts, per_device(): pl.pallas_call(modes_kernel, grid=(GROUPS,), out_shape=jax.ShapeDtypeStru...  9.88 us
    pallas_call x1, Pallas kernels, per_device(): pl.pallas_call(spectra_kernel, out_shape=(jax.ShapeDtypeStruct((2, FP, NB...  8.91 us
    pallas_call x1, Pallas kernels, per_device(): pl.pallas_call(modes_kernel, grid=(GROUPS,), out_shape=jax.ShapeDtypeStru...  7.17 us
    unnamed x12, local copies, waits for them, and re-layouts  5.97 us

profile of v1, /device:TPU:0, one launch (start us, length us, event | category | flops | bytes accessed | tf_op | source)
XLA Modules:
  0.0 108.2 jit_solution(3774622870826660808)
XLA Ops:
  0.0 0.0 copy-start.4
  0.0 0.0 copy-start.5
  0.0 1.8 %copy.8 = bf16[16,16,8,512]{3,2,0,1:T(8,128)(2,1)S(1)} copy(bf16[16,16,8,512]{3,2,1,0:T(8,128)(2,1)} %bitcast.14) | data formatting | bytes 4194304 | tf_op jit(solution)/shard_map/reshape | solution.py:225
  1.9 54.5 %all_to_all.15 = bf16[128,16,512]{2,0,1:T(8,128)(2,1)S(1)} all-to-all(bf16[128,16,512]{2,0,1:T(8,128)(2,1)S(1)} %bitcast.13), channel_id=1, replica_groups=mesh['slab'=2,'space'=16] {'space'}, dimensions={1} | all-to-all | bytes 4194304 | tf_op jit(solution)/shard_map/all_to_all | solution.py:226
  56.3 0.0 copy-done.4
  56.3 0.0 copy-done.5
  56.3 8.9 %spectra.1 = (bf16[2,136,16,512]{3,2,1,0:T(8,128)(2,1)S(1)}, f32[640,128]{1,0:T(8,128)S(1)}) custom-call(bf16[272,256]{1,0:T(8,128)(2,1)S(1)} %copy-done.4, bf16[2048,512]{1,0:T(8,128)(2,1)S(1)} %bitcast.10, f32[1,512]{1,0:T(1,128)S(1)} %bitcast.11), custom_call_target="tpu_custom_call" | custom-call | tf_op jit(solution)/shard_map/spectra/pallas_call | solution.py:230
  65.3 0.0 copy-start
  65.3 2.0 %copy-done = bf16[2,136,16,512]{3,2,1,0:T(8,128)(2,1)} copy-done((bf16[2,136,16,512]{3,2,1,0:T(8,128)(2,1)}, bf16[2,136,16,512]{3,2,1,0:T(8,128)(2,1)S(1)}, u32[]{:S(2)}) %copy-start) | copy-done | bytes 4456472
  67.3 0.0 copy-start.3
  67.3 0.7 copy-done.3
  68.0 19.8 %gram_sum.1.g_ref = f32[640,128]{1,0:T(8,128)} custom-call(f32[640,128]{1,0:T(8,128)} %copy-done.3), custom_call_target="tpu_custom_call" | custom-call | tf_op jit(solution)/shard_map/gram_sum/pallas_call | solution.py:242
  87.9 0.0 copy-start.1
  87.9 2.3 %copy-done.1 = bf16[2,136,16,512]{3,2,1,0:T(8,128)(2,1)S(1)} copy-done((bf16[2,136,16,512]{3,2,1,0:T(8,128)(2,1)S(1)}, bf16[2,136,16,512]{3,2,1,0:T(8,128)(2,1)}, u32[]{:S(2)}) %copy-start.1) | copy-done | bytes 4456472
  90.1 0.0 copy-start.2
  90.1 1.0 copy-done.2
  91.1 7.2 %modes.1 = bf16[2,129,15,512]{3,2,1,0:T(8,128)(2,1)S(1)} custom-call(f32[640,128]{1,0:T(8,128)S(1)} %copy-done.2, f32[1,512]{1,0:T(1,128)S(1)} %bitcast.12, bf16[2,136,16,512]{3,2,1,0:T(8,128)(2,1)S(1)} %copy-done.1), custom_call_target="tpu_custom_call" | custom-call | tf_op jit(solution)/shard_map/modes/pallas_call | solution.py:255
  98.3 9.9 %copy.5 = bf16[2,129,15,512]{3,0,2,1:T(2,128)(2,1)} copy(bf16[2,129,15,512]{3,2,1,0:T(8,128)(2,1)S(1)} %modes.1) | data formatting | bytes 7925760 | tf_op jit(solution)/shard_map/modes/pallas_call | solution.py:255
Async XLA Ops:
  0.0 56.3 %copy-start.4 = (bf16[272,256]{1,0:T(8,128)(2,1)S(1)}, bf16[272,256]{1,0:T(8,128)(2,1)}, u32[]{:S(2)}) copy-start(bf16[272,256]{1,0:T(8,128)(2,1)} %constant.2.clone.tab_ref) | copy-start | bytes 417796
  0.0 56.3 %copy-start.5 = (f32[512]{0:T(512)S(1)}, f32[512]{0:T(512)}, u32[]{:S(2)}) copy-start(f32[512]{0:T(512)} %param.4) | copy-start | bytes 6148
  65.3 2.0 %copy-start = (bf16[2,136,16,512]{3,2,1,0:T(8,128)(2,1)}, bf16[2,136,16,512]{3,2,1,0:T(8,128)(2,1)S(1)}, u32[]{:S(2)}) copy-start(bf16[2,136,16,512]{3,2,1,0:T(8,128)(2,1)S(1)} %get-tuple-element.8.wtd_ref) | copy-start | bytes 13369348
  67.3 0.7 copy-start.3
  87.9 2.3 %copy-start.1 = (bf16[2,136,16,512]{3,2,1,0:T(8,128)(2,1)S(1)}, bf16[2,136,16,512]{3,2,1,0:T(8,128)(2,1)}, u32[]{:S(2)}) copy-start(bf16[2,136,16,512]{3,2,1,0:T(8,128)(2,1)} %copy-done) | copy-start | bytes 13369348
  90.1 1.0 copy-start.2

commit v2 on v1

v2 whole, which is shorter than its diff:
```python
import functools
import math

import jax
import jax.numpy as jnp
import numpy as np
import ml_dtypes
from jax import lax
from jax.experimental import pallas as pl
from jax.experimental.pallas import tpu as pltpu
from jax.sharding import PartitionSpec as P

SEG = 256
HALF = SEG // 2
NB = 15
FREQS = 129
NBP = 16
GROUP = 8
GROUPS = -(-FREQS // GROUP)
FP = GROUPS * GROUP
LANES = 128
MESH = pl.DeviceIdType.MESH
VMEM = pl.BlockSpec(memory_space=pltpu.VMEM)


def make_table():
    t = np.arange(SEG)
    k = np.arange(FREQS)
    phases = 2.0 * np.pi * (k[:, None] * t[None, :] % SEG) / SEG
    taper = 0.5 - 0.5 * np.cos(2.0 * np.pi * t / SEG)
    scaling = 1.0 / math.sqrt(3.0 * SEG / 8.0)
    table = np.zeros((2, FP, SEG), np.float32)
    table[0, :FREQS] = taper * np.cos(phases) * scaling
    table[1, :FREQS] = -taper * np.sin(phases) * scaling
    return table.reshape(2 * FP, SEG).astype(ml_dtypes.bfloat16)


CHUNK = 256


def dft_chunk(tab_ref, x_ref, w_ref, s_ref, h):
    tab = tab_ref[...]
    row_sums = jnp.sum(tab.astype(jnp.float32), axis=1, keepdims=True)
    average = jnp.sum(x_ref[h].astype(jnp.float32), axis=0, keepdims=True) / x_ref.shape[1]
    root = jnp.sqrt(w_ref[:, pl.ds(pl.multiple_of(h * CHUNK, CHUNK), CHUNK)])
    corr = row_sums * (average * root)
    for b in range(NB):
        sp = jnp.dot(tab, x_ref[h, b * HALF : b * HALF + SEG, :], preferred_element_type=jnp.float32)
        sp = sp * root - corr
        for p in range(2):
            for i in range(CHUNK // LANES):
                s_ref[p, i, pl.ds(b, FP, stride=NBP), :] = sp[
                    p * FP : (p + 1) * FP, i * LANES : (i + 1) * LANES
                ]


def gram_group(s_ref, wtd_ref, g_ref, h, g):
    rows = pl.ds(pl.multiple_of(g * LANES, LANES), LANES)
    cols = pl.ds(pl.multiple_of(h * CHUNK, CHUNK), CHUNK)
    parts = [
        jnp.concatenate([s_ref[p, i, rows, :] for i in range(CHUNK // LANES)], axis=1).astype(jnp.bfloat16)
        for p in range(2)
    ]
    for p in range(2):
        wtd_ref[p, pl.ds(pl.multiple_of(g * GROUP, GROUP), GROUP), :, cols] = parts[p].reshape(
            GROUP, NBP, CHUNK
        )
    x = jnp.concatenate(parts, axis=0)
    prod = lax.dot_general(x, x, (((1,), (1,)), ((), ())), preferred_element_type=jnp.float32)
    re = prod[:LANES, :LANES] + prod[LANES:, LANES:]
    im = prod[:LANES, LANES:] - prod[LANES:, :LANES]
    freq = lax.broadcasted_iota(jnp.int32, (NBP, LANES), 1) // NBP
    for part, full in enumerate((re, im)):
        folded = jnp.zeros((NBP, LANES), jnp.float32)
        for k in range(GROUP):
            folded = jnp.where(freq == k, full[k * NBP : (k + 1) * NBP], folded)
        g_ref[g, part] += folded


def group_sum(x, lane):
    for step in (1, 2, 4, 8):
        x = x + jnp.take_along_axis(x, jnp.bitwise_xor(lane, step), axis=1)
    return x


def invert(re, im, real):
    shape = re.shape
    flat = (shape[0] * NBP, LANES)
    row = lax.broadcasted_iota(jnp.int32, (1, NBP, LANES), 1)
    lane = lax.broadcasted_iota(jnp.int32, (1, NBP, LANES), 2)
    col = lane % NBP
    lane_flat = lax.broadcasted_iota(jnp.int32, flat, 1)
    base = lane_flat - lane_flat % NBP
    diag = row == col
    trace = jnp.sum(jnp.where(diag, re, 0.0), axis=1, keepdims=True)
    level = group_sum(jnp.broadcast_to(trace, shape).reshape(flat), lane_flat).reshape(shape) / NB
    level = jnp.where(real, level, 1.0)
    re = re + jnp.where(diag, level, 0.0)
    for j in range(NB):
        index = base + j
        col_re = jnp.take_along_axis(re.reshape(flat), index, axis=1).reshape(shape)
        col_im = jnp.take_along_axis(im.reshape(flat), index, axis=1).reshape(shape)
        inverse = 1.0 / col_re[:, j : j + 1]
        here = (col == j)[:, j : j + 1]
        row_re = jnp.where(here, inverse, re[:, j : j + 1] * inverse)
        row_im = jnp.where(here, 0.0, im[:, j : j + 1] * inverse)
        cross = (row == j) | (col == j)
        col_re = jnp.where(row == j, -1.0, col_re)
        col_im = jnp.where(row == j, 0.0, col_im)
        re = jnp.where(cross, 0.0, re) - (col_re * row_re - col_im * row_im)
        im = jnp.where(cross, 0.0, im) - (col_re * row_im + col_im * row_re)
    return jnp.where(diag, 1.0, 0.0) - level * re, level * im


def filters_kernel(
    n, snap_ref, tab_ref, w_ref, wtd_ref, f_ref,
    x_ref, s_ref, g_ref, got_ref, tot_ref,
    x_own, x_send, x_recv, g_send, g_recv, f_send, f_recv,
):
    me = lax.axis_index("space")
    rows = snap_ref.shape[0]
    cells = w_ref.shape[1]
    pieces = cells // CHUNK
    slots = -(-GROUPS // n)

    def peer(i):
        return lax.rem(me + i, n)

    def piece(there, h):
        return snap_ref.at[:, pl.ds(pl.multiple_of(there * cells + h * CHUNK, CHUNK), CHUNK)]

    x_mine = pl.ds(pl.multiple_of(me * rows, rows), rows)

    def local(h):
        return pltpu.make_async_copy(piece(me, h), x_ref.at[h, x_mine], x_own.at[h])

    def exchange(i, h):
        there = peer(i)
        return pltpu.make_async_remote_copy(
            src_ref=piece(there, h),
            dst_ref=x_ref.at[h, x_mine],
            send_sem=x_send.at[h, i],
            recv_sem=x_recv.at[h, i],
            device_id={"space": there},
            device_id_type=MESH,
        )

    def scatter(g):
        return pltpu.make_async_remote_copy(
            src_ref=g_ref.at[g],
            dst_ref=got_ref.at[g // n, me],
            send_sem=g_send.at[g],
            recv_sem=g_recv.at[g // n, me],
            device_id={"space": lax.rem(g, n)},
            device_id_type=MESH,
        )

    def scattered(slot, source):
        return pltpu.make_async_remote_copy(
            src_ref=g_ref.at[0],
            dst_ref=got_ref.at[slot, source],
            send_sem=g_send.at[0],
            recv_sem=g_recv.at[slot, source],
            device_id={"space": source},
            device_id_type=MESH,
        )

    def gather(g, i):
        return pltpu.make_async_remote_copy(
            src_ref=f_ref.at[g],
            dst_ref=f_ref.at[g],
            send_sem=f_send.at[g // n, i],
            recv_sem=f_recv.at[g],
            device_id={"space": peer(i)},
            device_id_type=MESH,
        )

    barrier = pltpu.get_barrier_semaphore()

    @pl.loop(1, n)
    def _(i):
        pl.semaphore_signal(barrier, inc=1, device_id={"space": peer(i)}, device_id_type=MESH)

    for h in range(pieces):
        local(h).start()
    pl.semaphore_wait(barrier, n - 1)

    @pl.loop(0, pieces)
    def _(h):
        @pl.loop(1, n)
        def _(i):
            exchange(i, h).start()

    g_ref[...] = jnp.zeros_like(g_ref)
    for p in range(2):
        for i in range(CHUNK // LANES):
            s_ref[p, i, pl.ds(NB, FP, stride=NBP), :] = jnp.zeros((FP, LANES), jnp.float32)

    @pl.loop(0, pieces)
    def _(h):
        @pl.loop(1, n)
        def _(i):
            exchange(i, h).wait_recv()

        local(h).wait()
        dft_chunk(tab_ref, x_ref, w_ref, s_ref, h)

        @pl.loop(0, GROUPS)
        def _(g):
            gram_group(s_ref, wtd_ref, g_ref, h, g)

            @pl.when(jnp.logical_and(h == pieces - 1, lax.rem(g, n) != me))
            def _():
                scatter(g).start()

    for slot in range(slots):
        g = slot * n + me

        @pl.when(g < GROUPS)
        def _():
            tot_ref[slot] = g_ref[g]

            @pl.loop(1, n)
            def _(i):
                source = peer(i)
                scattered(slot, source).wait_recv()
                tot_ref[slot] += got_ref[slot, source]

        @pl.when(g >= GROUPS)
        def _():
            tot_ref[slot] = jnp.zeros((2, NBP, LANES), jnp.float32)

    shape = (slots, NBP, LANES)
    freq = (lax.broadcasted_iota(jnp.int32, shape, 0) * n + me) * GROUP + lax.broadcasted_iota(
        jnp.int32, shape, 2
    ) // NBP
    same, other = invert(tot_ref[:, 0], tot_ref[:, 1], freq < FREQS)
    for slot in range(slots):
        g = slot * n + me

        @pl.when(g < GROUPS)
        def _():
            f_ref[g, 0] = same[slot].astype(jnp.bfloat16)
            f_ref[g, 1] = other[slot].astype(jnp.bfloat16)

            @pl.loop(1, n)
            def _(i):
                gather(g, i).start()

    @pl.loop(0, pieces)
    def _(h):
        @pl.loop(1, n)
        def _(i):
            exchange(i, h).wait_send()

    @pl.loop(0, GROUPS)
    def _(g):
        @pl.when(lax.rem(g, n) != me)
        def _():
            scatter(g).wait_send()
            gather(g, 0).wait_recv()

    for slot in range(slots):
        g = slot * n + me

        @pl.when(g < GROUPS)
        def _():
            @pl.loop(1, n)
            def _(i):
                gather(g, i).wait_send()


def modes_kernel(f_ref, w_ref, wtd_ref, out_ref, mix_ref):
    cells = w_ref.shape[1]
    inverse_root = 1.0 / jnp.sqrt(w_ref[...])
    own = (
        lax.broadcasted_iota(jnp.int32, (LANES, LANES), 0) // NBP
        == lax.broadcasted_iota(jnp.int32, (LANES, LANES), 1) // NBP
    )
    same, other = (
        jnp.where(own, jnp.concatenate([f_ref[0, part].astype(jnp.float32)] * GROUP, axis=0), 0.0)
        for part in range(2)
    )
    mix_ref[0, pl.ds(0, LANES, stride=2), :] = same
    mix_ref[0, pl.ds(1, LANES, stride=2), :] = -other
    mix_ref[1, pl.ds(0, LANES, stride=2), :] = other
    mix_ref[1, pl.ds(1, LANES, stride=2), :] = same
    filters = jnp.concatenate((mix_ref[0], mix_ref[1]), axis=1).astype(jnp.bfloat16)
    wtd = wtd_ref[...].reshape(2 * LANES, cells)
    mixed = jnp.dot(filters, wtd, preferred_element_type=jnp.float32) * inverse_root
    mixed = mixed.astype(jnp.bfloat16).reshape(GROUP, NBP, 2, cells)
    out_ref[...] = mixed[:, :NB]


def per_device(snapshots, weights):
    n = lax.axis_size("space")
    rows = snapshots.shape[0]
    cells = snapshots.shape[1] // n
    pieces = cells // CHUNK
    slots = -(-GROUPS // n)
    table = jnp.asarray(make_table())
    w = weights.reshape(1, cells)
    dma = pltpu.SemaphoreType.DMA
    wtd, filters = pl.pallas_call(
        functools.partial(filters_kernel, n),
        out_shape=(
            jax.ShapeDtypeStruct((2, FP, NBP, cells), jnp.bfloat16),
            jax.ShapeDtypeStruct((GROUPS, 2, NBP, LANES), jnp.bfloat16),
        ),
        in_specs=[pl.BlockSpec(memory_space=pl.ANY), VMEM, VMEM],
        out_specs=(VMEM, VMEM),
        scratch_shapes=[
            pltpu.VMEM((pieces, n * rows, CHUNK), jnp.bfloat16),
            pltpu.VMEM((2, CHUNK // LANES, FP * NBP, LANES), jnp.float32),
            pltpu.VMEM((GROUPS, 2, NBP, LANES), jnp.float32),
            pltpu.VMEM((slots, n, 2, NBP, LANES), jnp.float32),
            pltpu.VMEM((slots, 2, NBP, LANES), jnp.float32),
            dma((pieces,)),
            dma((pieces, n)),
            dma((pieces, n)),
            dma((GROUPS,)),
            dma((slots, n)),
            dma((slots, n)),
            dma((GROUPS,)),
        ],
        compiler_params=pltpu.CompilerParams(
            collective_id=0, has_side_effects=True, vmem_limit_bytes=40 << 20
        ),
        name="filters",
    )(snapshots, table, w)
    modes = pl.pallas_call(
        modes_kernel,
        grid=(GROUPS,),
        out_shape=jax.ShapeDtypeStruct((FREQS, NB, 2, cells), jnp.bfloat16),
        in_specs=[
            pl.BlockSpec((1, 2, NBP, LANES), lambda g: (g, 0, 0, 0)),
            VMEM,
            pl.BlockSpec((2, GROUP, NBP, cells), lambda g: (0, g, 0, 0)),
        ],
        out_specs=pl.BlockSpec((GROUP, NB, 2, cells), lambda g: (g, 0, 0, 0)),
        scratch_shapes=[pltpu.VMEM((2, 2 * LANES, LANES), jnp.float32)],
        compiler_params=pltpu.CompilerParams(vmem_limit_bytes=32 << 20),
        name="modes",
    )(filters, w, wtd)
    return modes.transpose(2, 0, 1, 3)


def solution(mesh):
    return jax.shard_map(
        per_device,
        mesh=mesh,
        in_specs=(P("space", "slab"), P(("slab", "space"))),
        out_specs=P(None, None, None, ("slab", "space")),
        check_vma=False,
    )
```

time: 109 us -> 84.3 us (0.77)
  blocking collectives: 54.5 us -> 0 us
  Pallas kernels: 35.9 us -> 80.9 us
  local copies, waits for them, and re-layouts: 17.7 us -> 3.18 us
    all_to_all x1 -> x0, blocking collectives: 54.5 us -> none  [per_device(): lax.all_to_all(shaped, 'space', split_axis=1, concat_axis=0, tiled=True)]
    pallas_call x2 -> x1, Pallas kernels: 28.8 us -> 72.5 us  [per_device(): pl.pallas_call(functools.partial(filters_kernel, n), out_shape=(jax.Shape...]
    pallas_call x1 -> x0, local copies, waits for them, and re-layouts: 9.88 us -> none  [per_device(): pl.pallas_call(modes_kernel, grid=(GROUPS,), out_shape=jax.ShapeDtypeStru...]
    unnamed x12 -> x6, local copies, waits for them, and re-layouts: 5.97 us -> 3.18 us
    reshape x1 -> x0, local copies, waits for them, and re-layouts: 1.84 us -> none  [per_device(): shaped = snapshots.reshape(snapshots.shape[0], n, cells)]
    pallas_call x1, Pallas kernels: 7.17 us -> 8.44 us  [per_device(): pl.pallas_call(modes_kernel, grid=(GROUPS,), out_shape=jax.ShapeDtypeStru...]
where the time goes in v2:
time: 84.3 us; the launch traced here: 84.1 us
  Pallas kernels  80.9 us (96%)
  local copies, waits for them, and re-layouts  3.18 us (4%)
    pallas_call x1, Pallas kernels, per_device(): pl.pallas_call(functools.partial(filters_kernel, n), out_shape=(jax.Shape...  72.5 us
    pallas_call x1, Pallas kernels, per_device(): pl.pallas_call(modes_kernel, grid=(GROUPS,), out_shape=jax.ShapeDtypeStru...  8.44 us
    unnamed x6, local copies, waits for them, and re-layouts  3.18 us

profile of v2, /device:TPU:0, one launch (start us, length us, event | category | flops | bytes accessed | tf_op | source)
XLA Modules:
  0.0 84.1 jit_solution(12762334942324841432)
XLA Ops:
  0.0 0.0 copy-start
  0.0 1.6 %copy-done = bf16[128,8192]{1,0:T(8,128)(2,1)S(1)} copy-done((bf16[128,8192]{1,0:T(8,128)(2,1)S(1)}, bf16[128,8192]{1,0:T(8,128)(2,1)}, u32[]{:S(2)}) %copy-start) | copy-done | bytes 2097176
  1.6 0.0 copy-start.1
  1.6 0.9 %copy-done.1 = bf16[272,256]{1,0:T(8,128)(2,1)S(1)} copy-done((bf16[272,256]{1,0:T(8,128)(2,1)S(1)}, bf16[272,256]{1,0:T(8,128)(2,1)}, u32[]{:S(2)}) %copy-start.1) | copy-done | bytes 139288
  2.5 0.0 copy-start.2
  2.5 0.7 copy-done.2
  3.2 72.5 %filters.1 = (bf16[2,136,16,512]{3,2,1,0:T(8,128)(2,1)S(1)}, bf16[17,2,16,128]{3,2,1,0:T(8,128)(2,1)S(1)}) custom-call(bf16[128,8192]{1,0:T(8,128)(2,1)S(1)} %copy-done, bf16[272,256]{1,0:T(8,128)(2,1)S(1)} %copy-done.1, f32[1,512]{1,0:T(1,128)S(1)} %bitcast.2), custom_call_target="tpu_custom_call" | custom-call | tf_op jit(solution)/shard_map/filters/pallas_call | solution.py:304
  75.6 8.4 %modes.1 = bf16[129,15,2,512]{3,2,1,0:T(2,128)(2,1)} custom-call(bf16[17,2,16,128]{3,2,1,0:T(8,128)(2,1)S(1)} %get-tuple-element.7.f_ref, f32[1,512]{1,0:T(1,128)S(1)} %bitcast.3, bf16[2,136,16,512]{3,2,1,0:T(8,128)(2,1)S(1)} %get-tuple-element.8.wtd_ref), custom_call_target="tpu_custom_call" | custom-call | tf_op jit(solution)/shard_map/modes/pallas_call | solution.py:331
Async XLA Ops:
  0.0 1.6 %copy-start = (bf16[128,8192]{1,0:T(8,128)(2,1)S(1)}, bf16[128,8192]{1,0:T(8,128)(2,1)}, u32[]{:S(2)}) copy-start(bf16[128,8192]{1,0:T(8,128)(2,1)} %snap_ref.1) | copy-start | bytes 6291460
  1.6 0.9 %copy-start.1 = (bf16[272,256]{1,0:T(8,128)(2,1)S(1)}, bf16[272,256]{1,0:T(8,128)(2,1)}, u32[]{:S(2)}) copy-start(bf16[272,256]{1,0:T(8,128)(2,1)} %constant.2.clone.tab_ref) | copy-start | bytes 417796
  2.5 0.7 copy-start.2

commit v3 on v2

--- a/solution.py
+++ b/solution.py
@@ -35,6 +35,8 @@
     return table.reshape(2 * FP, SEG).astype(ml_dtypes.bfloat16)
 
 
+VLIM = 60
+GS = 6
 CHUNK = 256
 
 
@@ -56,25 +58,46 @@
 
 def gram_group(s_ref, wtd_ref, g_ref, h, g):
     rows = pl.ds(pl.multiple_of(g * LANES, LANES), LANES)
-    cols = pl.ds(pl.multiple_of(h * CHUNK, CHUNK), CHUNK)
     parts = [
         jnp.concatenate([s_ref[p, i, rows, :] for i in range(CHUNK // LANES)], axis=1).astype(jnp.bfloat16)
         for p in range(2)
     ]
     for p in range(2):
-        wtd_ref[p, pl.ds(pl.multiple_of(g * GROUP, GROUP), GROUP), :, cols] = parts[p].reshape(
+        wtd_ref[h, p, pl.ds(pl.multiple_of(g * GROUP, GROUP), GROUP)] = parts[p].reshape(
             GROUP, NBP, CHUNK
         )
     x = jnp.concatenate(parts, axis=0)
     prod = lax.dot_general(x, x, (((1,), (1,)), ((), ())), preferred_element_type=jnp.float32)
     re = prod[:LANES, :LANES] + prod[LANES:, LANES:]
     im = prod[:LANES, LANES:] - prod[LANES:, :LANES]
+    row = lax.broadcasted_iota(jnp.int32, (LANES, LANES), 0) % NBP
+    col = lax.broadcasted_iota(jnp.int32, (LANES, LANES), 1) % NBP
+    g_ref[g] += fold(jnp.where(row <= col, re, im))
+
+
+def own_frequency():
+    return (
+        lax.broadcasted_iota(jnp.int32, (LANES, LANES), 0) // NBP
+        == lax.broadcasted_iota(jnp.int32, (LANES, LANES), 1) // NBP
+    )
+
+
+def fold(full):
     freq = lax.broadcasted_iota(jnp.int32, (NBP, LANES), 1) // NBP
-    for part, full in enumerate((re, im)):
-        folded = jnp.zeros((NBP, LANES), jnp.float32)
-        for k in range(GROUP):
-            folded = jnp.where(freq == k, full[k * NBP : (k + 1) * NBP], folded)
-        g_ref[g, part] += folded
+    folded = full[:NBP]
+    for k in range(1, GROUP):
+        folded = jnp.where(freq == k, full[k * NBP : (k + 1) * NBP], folded)
+    return folded
+
+
+def spread(folded):
+    return jnp.where(own_frequency(), jnp.concatenate([folded] * GROUP, axis=0), 0.0)
+
+
+def unpack(packed, swapped, row, col):
+    re = jnp.where(row <= col, packed, swapped)
+    im = jnp.where(row > col, packed, jnp.where(row < col, -swapped, 0.0))
+    return re, im
 
 
 def group_sum(x, lane):
@@ -113,7 +136,8 @@
 
 
 def filters_kernel(
-    n, snap_ref, tab_ref, w_ref, wtd_ref, f_ref,
+    n, snap_ref, tab_hbm, w_hbm, wtd_hbm, f_ref,
+    tab_ref, w_ref, wtd_ref, own_sem, wtd_sem,
     x_ref, s_ref, g_ref, got_ref, tot_ref,
     x_own, x_send, x_recv, g_send, g_recv, f_send, f_recv,
 ):
@@ -133,6 +157,10 @@
 
     def local(h):
         return pltpu.make_async_copy(piece(me, h), x_ref.at[h, x_mine], x_own.at[h])
+
+    def write(h):
+        cols = pl.ds(pl.multiple_of(h * CHUNK, CHUNK), CHUNK)
+        return pltpu.make_async_copy(wtd_ref.at[h], wtd_hbm.at[:, :, :, cols], wtd_sem.at[h])
 
     def exchange(i, h):
         there = peer(i)
@@ -191,10 +219,19 @@
         def _(i):
             exchange(i, h).start()
 
+    constants = (
+        pltpu.make_async_copy(tab_hbm, tab_ref, own_sem.at[0]),
+        pltpu.make_async_copy(w_hbm, w_ref, own_sem.at[1]),
+    )
+    for copy in constants:
+        copy.start()
     g_ref[...] = jnp.zeros_like(g_ref)
     for p in range(2):
         for i in range(CHUNK // LANES):
             s_ref[p, i, pl.ds(NB, FP, stride=NBP), :] = jnp.zeros((FP, LANES), jnp.float32)
+
+    for copy in constants:
+        copy.wait()
 
     @pl.loop(0, pieces)
     def _(h):
@@ -205,13 +242,15 @@
         local(h).wait()
         dft_chunk(tab_ref, x_ref, w_ref, s_ref, h)
 
-        @pl.loop(0, GROUPS)
+        @pl.loop(0, GROUPS, unroll=GROUPS)
         def _(g):
             gram_group(s_ref, wtd_ref, g_ref, h, g)
 
             @pl.when(jnp.logical_and(h == pieces - 1, lax.rem(g, n) != me))
             def _():
                 scatter(g).start()
+
+        write(h).start()
 
     for slot in range(slots):
         g = slot * n + me
@@ -228,20 +267,23 @@
 
         @pl.when(g >= GROUPS)
         def _():
-            tot_ref[slot] = jnp.zeros((2, NBP, LANES), jnp.float32)
+            tot_ref[slot] = jnp.zeros((NBP, LANES), jnp.float32)
 
     shape = (slots, NBP, LANES)
     freq = (lax.broadcasted_iota(jnp.int32, shape, 0) * n + me) * GROUP + lax.broadcasted_iota(
         jnp.int32, shape, 2
     ) // NBP
-    same, other = invert(tot_ref[:, 0], tot_ref[:, 1], freq < FREQS)
+    row = lax.broadcasted_iota(jnp.int32, (1, NBP, LANES), 1)
+    col = lax.broadcasted_iota(jnp.int32, (1, NBP, LANES), 2) % NBP
+    swapped = jnp.stack([fold(spread(tot_ref[slot]).T) for slot in range(slots)])
+    same, other = invert(*unpack(tot_ref[...], swapped, row, col), freq < FREQS)
+    filters = jnp.where(row <= col, same, other).astype(jnp.bfloat16)
     for slot in range(slots):
         g = slot * n + me
 
         @pl.when(g < GROUPS)
         def _():
-            f_ref[g, 0] = same[slot].astype(jnp.bfloat16)
-            f_ref[g, 1] = other[slot].astype(jnp.bfloat16)
+            f_ref[g] = filters[slot]
 
             @pl.loop(1, n)
             def _(i):
@@ -252,6 +294,8 @@
         @pl.loop(1, n)
         def _(i):
             exchange(i, h).wait_send()
+
+        write(h).wait()
 
     @pl.loop(0, GROUPS)
     def _(g):
@@ -272,24 +316,26 @@
 
 def modes_kernel(f_ref, w_ref, wtd_ref, out_ref, mix_ref):
     cells = w_ref.shape[1]
+    tiles = cells // LANES
     inverse_root = 1.0 / jnp.sqrt(w_ref[...])
-    own = (
-        lax.broadcasted_iota(jnp.int32, (LANES, LANES), 0) // NBP
-        == lax.broadcasted_iota(jnp.int32, (LANES, LANES), 1) // NBP
-    )
-    same, other = (
-        jnp.where(own, jnp.concatenate([f_ref[0, part].astype(jnp.float32)] * GROUP, axis=0), 0.0)
-        for part in range(2)
-    )
-    mix_ref[0, pl.ds(0, LANES, stride=2), :] = same
-    mix_ref[0, pl.ds(1, LANES, stride=2), :] = -other
-    mix_ref[1, pl.ds(0, LANES, stride=2), :] = other
-    mix_ref[1, pl.ds(1, LANES, stride=2), :] = same
-    filters = jnp.concatenate((mix_ref[0], mix_ref[1]), axis=1).astype(jnp.bfloat16)
-    wtd = wtd_ref[...].reshape(2 * LANES, cells)
-    mixed = jnp.dot(filters, wtd, preferred_element_type=jnp.float32) * inverse_root
-    mixed = mixed.astype(jnp.bfloat16).reshape(GROUP, NBP, 2, cells)
-    out_ref[...] = mixed[:, :NB]
+    row = lax.broadcasted_iota(jnp.int32, (LANES, LANES), 0) % NBP
+    col = lax.broadcasted_iota(jnp.int32, (LANES, LANES), 1) % NBP
+    rows = 2 * tiles * NBP
+    for s in range(GS):
+        packed = spread(f_ref[s].astype(jnp.float32))
+        same, other = unpack(packed, packed.T, row, col)
+        filters = jnp.concatenate(
+            (jnp.concatenate((same, other), axis=1), jnp.concatenate((-other, same), axis=1)), axis=0
+        ).astype(jnp.bfloat16)
+        wtd = wtd_ref[:, s * GROUP : (s + 1) * GROUP].reshape(2 * LANES, cells)
+        mixed = jnp.dot(filters, wtd, preferred_element_type=jnp.float32) * inverse_root
+        for q in range(2):
+            for i in range(tiles):
+                mix_ref[s, pl.ds(2 * i + q, LANES, stride=2 * tiles), :] = mixed[
+                    q * LANES : (q + 1) * LANES, i * LANES : (i + 1) * LANES
+                ]
+        for k in range(GROUP):
+            out_ref[s * GROUP + k] = mix_ref[s, k * rows : k * rows + 2 * tiles * NB, :].astype(jnp.bfloat16)
 
 
 def per_device(snapshots, weights):
@@ -297,6 +343,7 @@
     rows = snapshots.shape[0]
     cells = snapshots.shape[1] // n
     pieces = cells // CHUNK
+    tiles = cells // LANES
     slots = -(-GROUPS // n)
     table = jnp.asarray(make_table())
     w = weights.reshape(1, cells)
@@ -305,16 +352,21 @@
         functools.partial(filters_kernel, n),
         out_shape=(
             jax.ShapeDtypeStruct((2, FP, NBP, cells), jnp.bfloat16),
-            jax.ShapeDtypeStruct((GROUPS, 2, NBP, LANES), jnp.bfloat16),
+            jax.ShapeDtypeStruct((GROUPS, NBP, LANES), jnp.bfloat16),
         ),
-        in_specs=[pl.BlockSpec(memory_space=pl.ANY), VMEM, VMEM],
-        out_specs=(VMEM, VMEM),
+        in_specs=[pl.BlockSpec(memory_space=pltpu.HBM)] * 3,
+        out_specs=(pl.BlockSpec(memory_space=pl.ANY), VMEM),
         scratch_shapes=[
+            pltpu.VMEM(table.shape, table.dtype),
+            pltpu.VMEM(w.shape, w.dtype),
+            pltpu.VMEM((pieces, 2, FP, NBP, CHUNK), jnp.bfloat16),
+            dma((2,)),
+            dma((pieces,)),
             pltpu.VMEM((pieces, n * rows, CHUNK), jnp.bfloat16),
             pltpu.VMEM((2, CHUNK // LANES, FP * NBP, LANES), jnp.float32),
-            pltpu.VMEM((GROUPS, 2, NBP, LANES), jnp.float32),
-            pltpu.VMEM((slots, n, 2, NBP, LANES), jnp.float32),
-            pltpu.VMEM((slots, 2, NBP, LANES), jnp.float32),
+            pltpu.VMEM((GROUPS, NBP, LANES), jnp.float32),
+            pltpu.VMEM((slots, n, NBP, LANES), jnp.float32),
+            pltpu.VMEM((slots, NBP, LANES), jnp.float32),
             dma((pieces,)),
             dma((pieces, n)),
             dma((pieces, n)),
@@ -324,25 +376,26 @@
             dma((GROUPS,)),
         ],
         compiler_params=pltpu.CompilerParams(
-            collective_id=0, has_side_effects=True, vmem_limit_bytes=40 << 20
+            collective_id=0, has_side_effects=True, vmem_limit_bytes=VLIM << 20
         ),
         name="filters",
     )(snapshots, table, w)
     modes = pl.pallas_call(
         modes_kernel,
-        grid=(GROUPS,),
-        out_shape=jax.ShapeDtypeStruct((FREQS, NB, 2, cells), jnp.bfloat16),
+        grid=(-(-GROUPS // GS),),
+        out_shape=jax.ShapeDtypeStruct((FREQS, 2 * tiles * NB, LANES), jnp.bfloat16),
         in_specs=[
-            pl.BlockSpec((1, 2, NBP, LANES), lambda g: (g, 0, 0, 0)),
+            pl.BlockSpec((GS, NBP, LANES), lambda g: (g, 0, 0)),
             VMEM,
-            pl.BlockSpec((2, GROUP, NBP, cells), lambda g: (0, g, 0, 0)),
+            pl.BlockSpec((2, GS * GROUP, NBP, cells), lambda g: (0, g, 0, 0)),
         ],
-        out_specs=pl.BlockSpec((GROUP, NB, 2, cells), lambda g: (g, 0, 0, 0)),
-        scratch_shapes=[pltpu.VMEM((2, 2 * LANES, LANES), jnp.float32)],
-        compiler_params=pltpu.CompilerParams(vmem_limit_bytes=32 << 20),
+        out_specs=pl.BlockSpec((GS * GROUP, 2 * tiles * NB, LANES), lambda g: (g, 0, 0)),
+        scratch_shapes=[pltpu.VMEM((GS, 2 * tiles * LANES, LANES), jnp.float32)],
+        compiler_params=pltpu.CompilerParams(vmem_limit_bytes=VLIM << 20),
         name="modes",
     )(filters, w, wtd)
-    return modes.transpose(2, 0, 1, 3)
+    modes = modes.reshape(FREQS, NB, tiles, 2, LANES)
+    return modes.transpose(3, 0, 1, 2, 4).reshape(2, FREQS, NB, cells)
 
 
 def solution(mesh):

time: 84.3 us -> 77.2 us (0.916)
  Pallas kernels: 80.9 us -> 77.1 us
  local copies, waits for them, and re-layouts: 3.18 us -> 0 us
    unnamed x6 -> x0, local copies, waits for them, and re-layouts: 3.18 us -> none
    pallas_call x1, Pallas kernels: 8.44 us -> 6.23 us  [per_device(): pl.pallas_call(modes_kernel, grid=(-(-GROUPS // GS),), out_shape=jax.Shap...]
    pallas_call x1, Pallas kernels: 72.5 us -> 70.8 us  [per_device(): pl.pallas_call(functools.partial(filters_kernel, n), out_shape=(jax.Shape...]
where the time goes in v3:
time: 77.2 us; the launch traced here: 77.1 us
  Pallas kernels  77.1 us (100%)
    pallas_call x1, Pallas kernels, per_device(): pl.pallas_call(functools.partial(filters_kernel, n), out_shape=(jax.Shape...  70.8 us
    pallas_call x1, Pallas kernels, per_device(): pl.pallas_call(modes_kernel, grid=(-(-GROUPS // GS),), out_shape=jax.Shap...  6.23 us

profile of v3, /device:TPU:0, one launch (start us, length us, event | category | flops | bytes accessed | tf_op | source)
XLA Modules:
  0.0 77.1 jit_solution(11905739213724876271)
XLA Ops:
  0.0 70.8 %filters.1 = (bf16[2,136,16,512]{3,2,1,0:T(8,128)(2,1)}, bf16[17,16,128]{2,1,0:T(8,128)(2,1)}) custom-call(bf16[128,8192]{1,0:T(8,128)(2,1)} %snap_ref.1, bf16[272,256]{1,0:T(8,128)(2,1)} %constant.2.clone.tab_hbm, f32[1,512]{1,0:T(1,128)} %bitcast.6), custom_call_target="tpu_custom_call" | custom-call | tf_op jit(solution)/shard_map/filters/pallas_call | solution.py:351
  70.8 6.2 %modes.1 = bf16[129,120,128]{2,1,0:T(8,128)(2,1)} custom-call(bf16[17,16,128]{2,1,0:T(8,128)(2,1)} %get-tuple-element.7.f_ref, f32[1,512]{1,0:T(1,128)} %bitcast.7, bf16[2,136,16,512]{3,2,1,0:T(8,128)(2,1)} %get-tuple-element.8.wtd_ref), custom_call_target="tpu_custom_call" | custom-call | tf_op jit(solution)/shard_map/modes/pallas_call | solution.py:383

commit v4 on v3

--- a/solution.py
+++ b/solution.py
@@ -36,8 +36,8 @@
 
 
 VLIM = 60
-GS = 6
-CHUNK = 256
+GS = 9
+CHUNK = 128
 
 
 def dft_chunk(tab_ref, x_ref, w_ref, s_ref, h):
@@ -246,11 +246,13 @@
         def _(g):
             gram_group(s_ref, wtd_ref, g_ref, h, g)
 
-            @pl.when(jnp.logical_and(h == pieces - 1, lax.rem(g, n) != me))
-            def _():
-                scatter(g).start()
-
         write(h).start()
+
+    @pl.loop(0, GROUPS)
+    def _(g):
+        @pl.when(lax.rem(g, n) != me)
+        def _():
+            scatter(g).start()
 
     for slot in range(slots):
         g = slot * n + me

time: 77.2 us -> 73.7 us (0.955)
  Pallas kernels: 77.1 us -> 73.6 us
    pallas_call x1, Pallas kernels: 70.8 us -> 67.9 us  [per_device(): pl.pallas_call(functools.partial(filters_kernel, n), out_shape=(jax.Shape...]
where the time goes in v4:
time: 73.7 us; the launch traced here: 73.6 us
  Pallas kernels  73.6 us (100%)
    pallas_call x1, Pallas kernels, per_device(): pl.pallas_call(functools.partial(filters_kernel, n), out_shape=(jax.Shape...  67.9 us
    pallas_call x1, Pallas kernels, per_device(): pl.pallas_call(modes_kernel, grid=(-(-GROUPS // GS),), out_shape=jax.Shap...  5.71 us

profile of v4, /device:TPU:0, one launch (start us, length us, event | category | flops | bytes accessed | tf_op | source)
XLA Modules:
  0.0 73.6 jit_solution(13340820751469974170)
XLA Ops:
  0.0 67.9 %filters.1 = (bf16[2,136,16,512]{3,2,1,0:T(8,128)(2,1)}, bf16[17,16,128]{2,1,0:T(8,128)(2,1)}) custom-call(bf16[128,8192]{1,0:T(8,128)(2,1)} %snap_ref.1, bf16[272,256]{1,0:T(8,128)(2,1)} %constant.2.clone.tab_hbm, f32[1,512]{1,0:T(1,128)} %bitcast.6), custom_call_target="tpu_custom_call" | custom-call | tf_op jit(solution)/shard_map/filters/pallas_call | solution.py:353
  67.9 5.7 %modes.1 = bf16[129,120,128]{2,1,0:T(8,128)(2,1)} custom-call(bf16[17,16,128]{2,1,0:T(8,128)(2,1)} %get-tuple-element.7.f_ref, f32[1,512]{1,0:T(1,128)} %bitcast.7, bf16[2,136,16,512]{3,2,1,0:T(8,128)(2,1)} %get-tuple-element.8.wtd_ref), custom_call_target="tpu_custom_call" | custom-call | tf_op jit(solution)/shard_map/modes/pallas_call | solution.py:385

commit v5 on v4

--- a/solution.py
+++ b/solution.py
@@ -136,8 +136,8 @@
 
 
 def filters_kernel(
-    n, snap_ref, tab_hbm, w_hbm, wtd_hbm, f_ref,
-    tab_ref, w_ref, wtd_ref, own_sem, wtd_sem,
+    n, snap_ref, tab_hbm, w_hbm, wtd_hbm, f_hbm,
+    tab_ref, w_ref, wtd_ref, f_ref, own_sem, wtd_sem, f_own,
     x_ref, s_ref, g_ref, got_ref, tot_ref,
     x_own, x_send, x_recv, g_send, g_recv, f_send, f_recv,
 ):
@@ -163,7 +163,7 @@
         return pltpu.make_async_copy(wtd_ref.at[h], wtd_hbm.at[:, :, :, cols], wtd_sem.at[h])
 
     def exchange(i, h):
-        there = peer(i)
+        there = peer((n + 1) // 2 + jnp.where(i % 2 == 1, (i - 1) // 2, -(i // 2)))
         return pltpu.make_async_remote_copy(
             src_ref=piece(there, h),
             dst_ref=x_ref.at[h, x_mine],
@@ -193,10 +193,13 @@
             device_id_type=MESH,
         )
 
+    def keep(slot):
+        return pltpu.make_async_copy(f_ref.at[slot], f_hbm.at[slot * n + me], f_own.at[slot])
+
     def gather(g, i):
         return pltpu.make_async_remote_copy(
-            src_ref=f_ref.at[g],
-            dst_ref=f_ref.at[g],
+            src_ref=f_ref.at[g // n],
+            dst_ref=f_hbm.at[g],
             send_sem=f_send.at[g // n, i],
             recv_sem=f_recv.at[g],
             device_id={"space": peer(i)},
@@ -285,7 +288,8 @@
 
         @pl.when(g < GROUPS)
         def _():
-            f_ref[g] = filters[slot]
+            f_ref[slot] = filters[slot]
+            keep(slot).start()
 
             @pl.loop(1, n)
             def _(i):
@@ -314,6 +318,8 @@
             @pl.loop(1, n)
             def _(i):
                 gather(g, i).wait_send()
+
+            keep(slot).wait()
 
 
 def modes_kernel(f_ref, w_ref, wtd_ref, out_ref, mix_ref):
@@ -357,13 +363,15 @@
             jax.ShapeDtypeStruct((GROUPS, NBP, LANES), jnp.bfloat16),
         ),
         in_specs=[pl.BlockSpec(memory_space=pltpu.HBM)] * 3,
-        out_specs=(pl.BlockSpec(memory_space=pl.ANY), VMEM),
+        out_specs=(pl.BlockSpec(memory_space=pl.ANY),) * 2,
         scratch_shapes=[
             pltpu.VMEM(table.shape, table.dtype),
             pltpu.VMEM(w.shape, w.dtype),
             pltpu.VMEM((pieces, 2, FP, NBP, CHUNK), jnp.bfloat16),
+            pltpu.VMEM((slots, NBP, LANES), jnp.bfloat16),
             dma((2,)),
             dma((pieces,)),
+            dma((slots,)),
             pltpu.VMEM((pieces, n * rows, CHUNK), jnp.bfloat16),
             pltpu.VMEM((2, CHUNK // LANES, FP * NBP, LANES), jnp.float32),
             pltpu.VMEM((GROUPS, NBP, LANES), jnp.float32),

time: 73.7 us -> 72.6 us (0.985)
  Pallas kernels: 73.6 us -> 72.4 us
    pallas_call x1, Pallas kernels: 67.9 us -> 66.7 us  [per_device(): pl.pallas_call(functools.partial(filters_kernel, n), out_shape=(jax.Shape...]
where the time goes in v5:
time: 72.6 us; the launch traced here: 72.4 us
  Pallas kernels  72.4 us (100%)
    pallas_call x1, Pallas kernels, per_device(): pl.pallas_call(functools.partial(filters_kernel, n), out_shape=(jax.Shape...  66.7 us
    pallas_call x1, Pallas kernels, per_device(): pl.pallas_call(modes_kernel, grid=(-(-GROUPS // GS),), out_shape=jax.Shap...  5.71 us

profile of v5, /device:TPU:0, one launch (start us, length us, event | category | flops | bytes accessed | tf_op | source)
XLA Modules:
  0.0 72.4 jit_solution(17751629275507513007)
XLA Ops:
  0.0 66.7 %filters.1 = (bf16[2,136,16,512]{3,2,1,0:T(8,128)(2,1)}, bf16[17,16,128]{2,1,0:T(8,128)(2,1)}) custom-call(bf16[128,8192]{1,0:T(8,128)(2,1)} %snap_ref.1, bf16[272,256]{1,0:T(8,128)(2,1)} %constant.2.clone.tab_hbm, f32[1,512]{1,0:T(1,128)} %bitcast.6), custom_call_target="tpu_custom_call" | custom-call | tf_op jit(solution)/shard_map/filters/pallas_call | solution.py:359
  66.7 5.7 %modes.1 = bf16[129,120,128]{2,1,0:T(8,128)(2,1)} custom-call(bf16[17,16,128]{2,1,0:T(8,128)(2,1)} %get-tuple-element.7.f_ref, f32[1,512]{1,0:T(1,128)} %bitcast.7, bf16[2,136,16,512]{3,2,1,0:T(8,128)(2,1)} %get-tuple-element.8.wtd_ref), custom_call_target="tpu_custom_call" | custom-call | tf_op jit(solution)/shard_map/modes/pallas_call | solution.py:393

commit v6 on v5

--- a/solution.py
+++ b/solution.py
@@ -373,7 +373,7 @@
             dma((pieces,)),
             dma((slots,)),
             pltpu.VMEM((pieces, n * rows, CHUNK), jnp.bfloat16),
-            pltpu.VMEM((2, CHUNK // LANES, FP * NBP, LANES), jnp.float32),
+            pltpu.VMEM((2, CHUNK // LANES, (FP + 1) * NBP, LANES), jnp.float32),
             pltpu.VMEM((GROUPS, NBP, LANES), jnp.float32),
             pltpu.VMEM((slots, n, NBP, LANES), jnp.float32),
             pltpu.VMEM((slots, NBP, LANES), jnp.float32),
@@ -400,7 +400,7 @@
             pl.BlockSpec((2, GS * GROUP, NBP, cells), lambda g: (0, g, 0, 0)),
         ],
         out_specs=pl.BlockSpec((GS * GROUP, 2 * tiles * NB, LANES), lambda g: (g, 0, 0)),
-        scratch_shapes=[pltpu.VMEM((GS, 2 * tiles * LANES, LANES), jnp.float32)],
+        scratch_shapes=[pltpu.VMEM((GS, 2 * tiles * (LANES + 1), LANES), jnp.float32)],
         compiler_params=pltpu.CompilerParams(vmem_limit_bytes=VLIM << 20),
         name="modes",
     )(filters, w, wtd)

time: 72.6 us -> 72.6 us (level)
  no operation moved by 1% of the time
where the time goes in v6:
time: 72.6 us; the launch traced here: 72.5 us
  Pallas kernels  72.5 us (100%)
    pallas_call x1, Pallas kernels, per_device(): pl.pallas_call(functools.partial(filters_kernel, n), out_shape=(jax.Shape...  66.7 us
    pallas_call x1, Pallas kernels, per_device(): pl.pallas_call(modes_kernel, grid=(-(-GROUPS // GS),), out_shape=jax.Shap...  5.73 us

profile of v6, /device:TPU:0, one launch (start us, length us, event | category | flops | bytes accessed | tf_op | source)
XLA Modules:
  0.0 72.5 jit_solution(3928149370645117986)
XLA Ops:
  0.0 66.7 %filters.1 = (bf16[2,136,16,512]{3,2,1,0:T(8,128)(2,1)}, bf16[17,16,128]{2,1,0:T(8,128)(2,1)}) custom-call(bf16[128,8192]{1,0:T(8,128)(2,1)} %snap_ref.1, bf16[272,256]{1,0:T(8,128)(2,1)} %constant.2.clone.tab_hbm, f32[1,512]{1,0:T(1,128)} %bitcast.6), custom_call_target="tpu_custom_call" | custom-call | tf_op jit(solution)/shard_map/filters/pallas_call | solution.py:359
  66.7 5.7 %modes.1 = bf16[129,120,128]{2,1,0:T(8,128)(2,1)} custom-call(bf16[17,16,128]{2,1,0:T(8,128)(2,1)} %get-tuple-element.7.f_ref, f32[1,512]{1,0:T(1,128)} %bitcast.7, bf16[2,136,16,512]{3,2,1,0:T(8,128)(2,1)} %get-tuple-element.8.wtd_ref), custom_call_target="tpu_custom_call" | custom-call | tf_op jit(solution)/shard_map/modes/pallas_call | solution.py:393
